TPU v7x, 32 devices: a whole 2x2x4 slice. The times are simulated.
32 devices in a mesh: groups: 2 (over x), chan: 8 (over z, y), tm: 2 (over core).
Axes of the slice: x: 2, y: 2, z: 4, core: 2. Of those that a mesh axis runs over, the one named last changes fastest.
Arguments:
- raw_strain: bfloat16 [2, 2560, 4096], P('tm', 'chan', 'groups'), parts along dimension 2
- fir_taps: float32 [64], replicated, may hold values from -0.75 to 0.75
- source_picks: int32 [16, 8, 2], P(('groups', 'chan')), parts along dimension 0, may hold values from -1 to 255, as said below
Outputs:
- correlation: float32 [201, 16, 4096], P(None, None, ('groups', 'chan', 'tm')), parts along dimension 2
There are 2 independent parts, one for each index of `groups`. A program takes and returns all parts, laid end to end along the dimension named above; an argument that names none is the same for every part. Nothing has to cross between parts.
Inputs may be any that keep to these rules, and one draw needn't show every extreme that they name: source_picks[s, o, p] is a channel of sender block s, counted within the block, sent to owner block o in slot p, or -1 for an empty slot; the picks of one sender for one owner are distinct and fill slots 0 up to a count of 0 to 2; in every draw one owner block receives 2 rows from every sender block.
All inputs are finite; a program needn't handle non-finite values.
Results may differ from a plain program's by a relative error of at most 0.004.
Values may be sent and summed in bfloat16 or wider, within the bound.
A program may use at most 192 MiB of HBM per device.

v0:
```python
import functools
import math

import jax
import jax.numpy as jnp
from jax import lax
from jax.experimental import pallas as pl
from jax.experimental.pallas import tpu as pltpu
from jax.sharding import PartitionSpec as P

DEC = 10
TAPS = 64
HALF_WIN = 64
MAXLAG = 100
LANES = 128
epsilon = 1e-05
MESH = pl.DeviceIdType.MESH


def split3(value):
    high = value.astype(jnp.bfloat16)
    rest = value - high.astype(jnp.float32)
    middle = rest.astype(jnp.bfloat16)
    low = (rest - middle.astype(jnp.float32)).astype(jnp.bfloat16)
    return high, middle, low


def exchange_kernel(
    n_chan, n_tm, raw_ref, taps_ref, picks_ref, normed_ref, ext_ref,
    send, recv, mags, picked, arrived, sems,
):
    n = n_chan * n_tm
    chan = lax.axis_index("chan")
    half = lax.axis_index("tm")
    me = chan * n_tm + half
    my_time = half * n_chan + chan

    def partner(step):
        other = lax.rem(me + step, n)
        return other, {"chan": other // n_tm, "tm": lax.rem(other, n_tm)}

    def source(step):
        other = lax.rem(me + n - step, n)
        return other, lax.rem(other, n_tm) * n_chan + other // n_tm

    barrier = pltpu.get_barrier_semaphore()
    for step in range(1, n):
        pl.semaphore_signal(barrier, inc=1, device_id=partner(step)[1], device_id_type=MESH)

    raw_rows = raw_ref.shape[1]
    own = raw_rows // DEC
    rows = send.shape[1]
    lead = lax.broadcasted_iota(jnp.int32, (rows, raw_rows), 0) * DEC + (DEC - 1)
    tap_index = lead - lax.broadcasted_iota(jnp.int32, (rows, raw_rows), 1)
    table = jnp.zeros((rows, raw_rows), jnp.float32)
    for tap in range(TAPS):
        table = jnp.where(tap_index == tap, taps_ref[tap], table)
    weights = jnp.concatenate(split3(table), axis=0)
    for block in range(n // 2):
        part = jnp.dot(
            weights, raw_ref[0, :, block * 2 * LANES : (block + 1) * 2 * LANES],
            preferred_element_type=jnp.float32,
        )
        part = part[:rows] + part[rows : 2 * rows] + part[2 * rows :]
        send[2 * block] = part[:, :LANES]
        send[2 * block + 1] = part[:, LANES:]

    pl.semaphore_wait(barrier, n - 1)

    def first(step):
        other, where = partner(step)
        return pltpu.make_async_remote_copy(
            src_ref=send.at[other], dst_ref=recv.at[my_time],
            send_sem=sems.at[0, step], recv_sem=sems.at[1, step],
            device_id=where, device_id_type=MESH,
        )

    def first_in(step):
        return pltpu.make_async_remote_copy(
            src_ref=send.at[0], dst_ref=recv.at[source(step)[1]],
            send_sem=sems.at[0, step], recv_sem=sems.at[1, step],
            device_id=partner(step)[1], device_id_type=MESH,
        )

    for step in range(1, n):
        first(step).start()
    recv[my_time] = send[me]

    samples = normed_ref.shape[0]
    mags[:HALF_WIN] = jnp.zeros((HALF_WIN, 3 * LANES), jnp.bfloat16)
    mags[HALF_WIN + samples :] = jnp.zeros((HALF_WIN, 3 * LANES), jnp.bfloat16)
    band_shape = (LANES, LANES + 2 * HALF_WIN)
    offset = lax.broadcasted_iota(jnp.int32, band_shape, 1) - lax.broadcasted_iota(
        jnp.int32, band_shape, 0
    )
    band = jnp.where((offset >= 0) & (offset <= 2 * HALF_WIN), 1.0, 0.0).astype(jnp.bfloat16)
    owners, slots = picks_ref.shape[1:]
    pick_rows = owners * slots
    row = lax.broadcasted_iota(jnp.int32, (pick_rows, LANES), 0)
    lane = lax.broadcasted_iota(jnp.int32, (pick_rows, LANES), 1) + half * LANES
    chosen = jnp.full((pick_rows, LANES), -1, jnp.int32)
    for owner in range(owners):
        for slot in range(slots):
            chosen = jnp.where(row == owner * slots + slot, picks_ref[0, owner, slot], chosen)
    onehot = jnp.where(chosen == lane, 1.0, 0.0).astype(jnp.bfloat16)

    for step in range(1, n):
        first_in(step).wait_recv()

    def decimated(slab):
        body = recv[slab, :own]
        if slab == 0:
            return body
        spill = recv[slab - 1, own:]
        return jnp.concatenate([body[: rows - own] + spill, body[rows - own :]], axis=0)

    for slab in range(n):
        value = jnp.concatenate(split3(jnp.abs(decimated(slab))), axis=1)
        mags[HALF_WIN + slab * own : HALF_WIN + (slab + 1) * own] = value

    per_tile = LANES // own
    for tile in range(samples // LANES):
        sums = jnp.dot(
            band, mags[tile * LANES : tile * LANES + band_shape[1]],
            preferred_element_type=jnp.float32,
        )
        running = sums[:, :LANES] + sums[:, LANES : 2 * LANES] + sums[:, 2 * LANES :]
        values = jnp.concatenate(
            [decimated(tile * per_tile + i) for i in range(per_tile)], axis=0
        )
        normed = (values / (running / (2 * HALF_WIN + 1) + epsilon)).astype(jnp.bfloat16)
        normed_ref[tile * LANES : (tile + 1) * LANES] = normed
        found = lax.dot_general(
            onehot, normed, (((1,), (1,)), ((), ())), preferred_element_type=jnp.float32
        )
        for owner in range(owners):
            picked[owner, tile * slots : (tile + 1) * slots] = found[
                owner * slots : (owner + 1) * slots
            ]

    def second(step):
        other, where = partner(step)
        return pltpu.make_async_remote_copy(
            src_ref=picked.at[other // n_tm], dst_ref=arrived.at[me],
            send_sem=sems.at[2, step], recv_sem=sems.at[3, step],
            device_id=where, device_id_type=MESH,
        )

    def second_in(step):
        return pltpu.make_async_remote_copy(
            src_ref=picked.at[0], dst_ref=arrived.at[source(step)[0]],
            send_sem=sems.at[2, step], recv_sem=sems.at[3, step],
            device_id=partner(step)[1], device_id_type=MESH,
        )

    for step in range(1, n):
        second(step).start()
    arrived[me] = picked[chan]
    ext_ref[...] = jnp.zeros_like(ext_ref)
    for step in range(1, n):
        second_in(step).wait_recv()
    for sender in range(n_chan):
        total = arrived[sender * n_tm]
        for other in range(1, n_tm):
            total = total + arrived[sender * n_tm + other]
        for tile in range(samples // LANES):
            ext_ref[
                sender * slots : (sender + 1) * slots, (tile + 1) * LANES : (tile + 2) * LANES
            ] = total[tile * slots : (tile + 1) * slots]
    for step in range(1, n):
        first(step).wait_send()
        second(step).wait_send()


def correlate_kernel(scale, ext_ref, normed_ref, out_ref):
    lags, slots, _ = out_ref.shape
    samples = normed_ref.shape[0]
    receivers = normed_ref[...]
    group = max(1, 128 // slots)
    for start in range(0, lags, group):
        stop = min(start + group, lags)
        windows = []
        for lag in range(start, stop):
            base = LANES + MAXLAG - lag
            windows.append(ext_ref[:, base : base + samples].astype(jnp.bfloat16))
        left = jnp.concatenate(windows, axis=0)
        found = jnp.dot(left, receivers, preferred_element_type=jnp.float32) * scale
        out_ref[start:stop] = found.reshape(stop - start, slots, LANES)


def per_device(n_chan, n_tm, raw_strain, fir_taps, source_picks):
    n = n_chan * n_tm
    own = raw_strain.shape[1] // DEC
    rows = own + 8
    samples = own * n
    slots = source_picks.shape[2]
    vmem = pl.BlockSpec(memory_space=pltpu.VMEM)
    smem = pl.BlockSpec(memory_space=pltpu.SMEM)
    normed, ext = pl.pallas_call(
        functools.partial(exchange_kernel, n_chan, n_tm),
        out_shape=(
            jax.ShapeDtypeStruct((samples, LANES), jnp.bfloat16),
            jax.ShapeDtypeStruct((n_chan * slots, samples + 2 * LANES), jnp.float32),
        ),
        in_specs=[vmem, smem, smem],
        out_specs=(vmem, vmem),
        scratch_shapes=[
            pltpu.VMEM((n, rows, LANES), jnp.float32),
            pltpu.VMEM((n, rows, LANES), jnp.float32),
            pltpu.VMEM((samples + 2 * HALF_WIN, 3 * LANES), jnp.bfloat16),
            pltpu.VMEM((n_chan, slots * samples // LANES, LANES), jnp.float32),
            pltpu.VMEM((n, slots * samples // LANES, LANES), jnp.float32),
            pltpu.SemaphoreType.DMA((4, n)),
        ],
        compiler_params=pltpu.CompilerParams(
            collective_id=0, has_side_effects=True, vmem_limit_bytes=40 * 2**20
        ),
    )(raw_strain, fir_taps, source_picks)
    return pl.pallas_call(
        functools.partial(correlate_kernel, 1.0 / math.sqrt(samples)),
        out_shape=jax.ShapeDtypeStruct((2 * MAXLAG + 1, n_chan * slots, LANES), jnp.float32),
        in_specs=[vmem, vmem],
        out_specs=vmem,
        compiler_params=pltpu.CompilerParams(vmem_limit_bytes=40 * 2**20),
    )(ext, normed)


def solution(mesh):
    placed = (P("tm", "chan", "groups"), P(), P(("groups", "chan"), None, None))
    return jax.shard_map(
        functools.partial(per_device, mesh.shape["chan"], mesh.shape["tm"]),
        mesh=mesh,
        in_specs=placed,
        out_specs=P(None, None, ("groups", "chan", "tm")),
        check_vma=False,
    )
```

profile of v0, /device:TPU:0, one launch (start us, length us, event | category | flops | bytes accessed | tf_op | source)
XLA Modules:
  0.0 28.5 jit_solution(2131839936832975827)
XLA Ops:
  0.0 0.8 %copy.4.picks_ref = s32[1,8,2]{2,1,0:T(8,128)S(1)} copy(s32[1,8,2]{1,2,0:T(2,128)} %param.5) | data formatting | bytes 128 | tf_op args[2]
  0.8 0.0 copy-start
  0.8 1.3 %copy-done = bf16[1,320,2048]{2,1,0:T(8,128)(2,1)S(1)} copy-done((bf16[1,320,2048]{2,1,0:T(8,128)(2,1)S(1)}, bf16[1,320,2048]{2,1,0:T(8,128)(2,1)}, u32[]{:S(2)}) %copy-start) | copy-done | bytes 1310744
  2.1 0.0 copy-start.1
  2.1 0.7 %copy-done.1 = f32[64]{0:T(128)S(1)} copy-done((f32[64]{0:T(128)S(1)}, f32[64]{0:T(128)}, u32[]{:S(2)}) %copy-start.1) | copy-done | bytes 280
  2.7 21.5 %shard_map.37 = (bf16[512,128]{1,0:T(8,128)(2,1)S(1)}, f32[16,768]{1,0:T(8,128)S(1)}) custom-call(bf16[1,320,2048]{2,1,0:T(8,128)(2,1)S(1)} %copy-done, f32[64]{0:T(128)S(1)} %copy-done.1, s32[1,8,2]{2,1,0:T(8,128)S(1)} %copy.4.picks_ref), custom_call_target="tpu_custom_call" | custom-call | tf_op jit(solution)/shard_map/pallas_call | solution.py:199
  24.2 4.3 %shard_map.38 = f32[201,16,128]{2,1,0:T(8,128)} custom-call(f32[16,768]{1,0:T(8,128)S(1)} %get-tuple-element.7.ext_ref, bf16[512,128]{1,0:T(8,128)(2,1)S(1)} %get-tuple-element.8.normed_ref), custom_call_target="tpu_custom_call" | custom-call | tf_op jit(solution)/shard_map/pallas_call | solution.py:219
Async XLA Ops:
  0.8 1.3 %copy-start = (bf16[1,320,2048]{2,1,0:T(8,128)(2,1)S(1)}, bf16[1,320,2048]{2,1,0:T(8,128)(2,1)}, u32[]{:S(2)}) copy-start(bf16[1,320,2048]{2,1,0:T(8,128)(2,1)} %raw_ref.1) | copy-start | bytes 3932164
  2.1 0.7 %copy-start.1 = (f32[64]{0:T(128)S(1)}, f32[64]{0:T(128)}, u32[]{:S(2)}) copy-start(f32[64]{0:T(128)} %taps_ref.1) | copy-start | bytes 772
where the time goes:
time: 28.7 us; the launch traced here: 28.5 us
  Pallas kernels  25.8 us (90%)
  local copies, waits for them, and re-layouts  2.72 us (9%)
    pallas_call x1, Pallas kernels, per_device(): pl.pallas_call(functools.partial(exchange_kernel, n_chan, n_tm), out_shap...  21.5 us
    pallas_call x1, Pallas kernels, per_device(): pl.pallas_call(functools.partial(correlate_kernel, 1.0 / math.sqrt(sample...  4.31 us
    unnamed x5, local copies, waits for them, and re-layouts  2.72 us

commit v1 on v0

v1 whole, which is shorter than its diff:
```python
import functools
import math

import jax
import jax.numpy as jnp
from jax import lax
from jax.experimental import pallas as pl
from jax.experimental.pallas import tpu as pltpu
from jax.sharding import PartitionSpec as P

DEC = 10
TAPS = 64
HALF_WIN = 64
MAXLAG = 100
LANES = 128
epsilon = 1e-05
MESH = pl.DeviceIdType.MESH


def split3(value):
    high = value.astype(jnp.bfloat16)
    rest = value - high.astype(jnp.float32)
    middle = rest.astype(jnp.bfloat16)
    low = (rest - middle.astype(jnp.float32)).astype(jnp.bfloat16)
    return high, middle, low


def exchange_kernel(
    n_chan, n_tm, raw_hbm, taps_hbm, picks_hbm, normed_ref, ext_ref,
    raw_ref, taps_ref, picks_ref, send, recv, mags, picked, arrived, wide, loads, sems,
):
    n = n_chan * n_tm
    chan = lax.axis_index("chan")
    half = lax.axis_index("tm")
    me = chan * n_tm + half
    my_time = half * n_chan + chan
    order = sorted(range(n_chan), key=lambda d: abs(2 * d - n_chan))
    steps = [(d, g) for d in order for g in range(n_tm) if d or g]
    block_width = n_tm * LANES

    def partner(d, g):
        return lax.rem(chan + d, n_chan), lax.rem(half + g, n_tm)

    def target(d, g):
        other_chan, other_half = partner(d, g)
        return {"chan": other_chan, "tm": other_half}

    def source(d, g):
        return lax.rem(chan + n_chan - d, n_chan), lax.rem(half + n_tm - g, n_tm)

    def load(d):
        column = pl.multiple_of(lax.rem(chan + d, n_chan) * block_width, block_width)
        return pltpu.make_async_copy(
            raw_hbm.at[0, :, pl.ds(column, block_width)], raw_ref.at[d], loads.at[d]
        )

    taps_copy = pltpu.make_async_copy(taps_hbm, taps_ref, loads.at[n_chan])
    picks_copy = pltpu.make_async_copy(picks_hbm, picks_ref, loads.at[n_chan + 1])
    taps_copy.start()
    for d in order:
        load(d).start()
    picks_copy.start()
    barrier = pltpu.get_barrier_semaphore()
    for d, g in steps:
        pl.semaphore_signal(barrier, inc=1, device_id=target(d, g), device_id_type=MESH)

    def first(d, g):
        index = d * n_tm + g
        return pltpu.make_async_remote_copy(
            src_ref=send.at[d * n_tm + partner(d, g)[1]], dst_ref=recv.at[my_time],
            send_sem=sems.at[0, index], recv_sem=sems.at[1, index],
            device_id=target(d, g), device_id_type=MESH,
        )

    def first_in(d, g):
        index = d * n_tm + g
        from_chan, from_half = source(d, g)
        return pltpu.make_async_remote_copy(
            src_ref=send.at[0], dst_ref=recv.at[from_half * n_chan + from_chan],
            send_sem=sems.at[0, index], recv_sem=sems.at[1, index],
            device_id=target(d, g), device_id_type=MESH,
        )

    raw_rows = raw_ref.shape[1]
    own = raw_rows // DEC
    rows = send.shape[1]
    lead = lax.broadcasted_iota(jnp.int32, (rows, raw_rows), 0) * DEC + (DEC - 1)
    tap_index = lead - lax.broadcasted_iota(jnp.int32, (rows, raw_rows), 1)
    table = jnp.zeros((rows, raw_rows), jnp.float32)
    taps_copy.wait()
    for tap in range(TAPS):
        table = jnp.where(tap_index == tap, taps_ref[tap], table)
    weights = jnp.concatenate(split3(table), axis=0)
    for place, d in enumerate(order):
        load(d).wait()
        part = jnp.dot(weights, raw_ref[d], preferred_element_type=jnp.float32)
        part = part[:rows] + part[rows : 2 * rows] + part[2 * rows :]
        for h in range(n_tm):
            send[d * n_tm + h] = part[:, h * LANES : (h + 1) * LANES]
        if place == 0:
            pl.semaphore_wait(barrier, n - 1)
        for g in range(n_tm):
            if d or g:
                first(d, g).start()
    recv[my_time] = send[half]
    picks_copy.wait()

    samples = normed_ref.shape[0]
    mags[:HALF_WIN] = jnp.zeros((HALF_WIN, 3 * LANES), jnp.bfloat16)
    mags[HALF_WIN + samples :] = jnp.zeros((HALF_WIN, 3 * LANES), jnp.bfloat16)
    band_shape = (LANES, LANES + 2 * HALF_WIN)
    offset = lax.broadcasted_iota(jnp.int32, band_shape, 1) - lax.broadcasted_iota(
        jnp.int32, band_shape, 0
    )
    band = jnp.where((offset >= 0) & (offset <= 2 * HALF_WIN), 1.0, 0.0).astype(jnp.bfloat16)
    slots, owners = picks_ref.shape[1:]
    pick_rows = owners * slots
    row = lax.broadcasted_iota(jnp.int32, (pick_rows, LANES), 0)
    lane = lax.broadcasted_iota(jnp.int32, (pick_rows, LANES), 1) + half * LANES
    chosen = jnp.full((pick_rows, LANES), -1, jnp.int32)
    for owner in range(owners):
        for slot in range(slots):
            chosen = jnp.where(row == owner * slots + slot, picks_ref[0, slot, owner], chosen)
    onehot = jnp.where(chosen == lane, 1.0, 0.0).astype(jnp.bfloat16)

    for d, g in steps:
        first_in(d, g).wait_recv()

    def decimated(slab):
        body = recv[slab, :own]
        if slab == 0:
            return body
        spill = recv[slab - 1, own:]
        return jnp.concatenate([body[: rows - own] + spill, body[rows - own :]], axis=0)

    for slab in range(n):
        value = jnp.concatenate(split3(jnp.abs(decimated(slab))), axis=1)
        mags[HALF_WIN + slab * own : HALF_WIN + (slab + 1) * own] = value

    per_tile = LANES // own
    for tile in range(samples // LANES):
        sums = jnp.dot(
            band, mags[tile * LANES : tile * LANES + band_shape[1]],
            preferred_element_type=jnp.float32,
        )
        running = sums[:, :LANES] + sums[:, LANES : 2 * LANES] + sums[:, 2 * LANES :]
        values = jnp.concatenate(
            [decimated(tile * per_tile + i) for i in range(per_tile)], axis=0
        )
        normed = (values / (running / (2 * HALF_WIN + 1) + epsilon)).astype(jnp.bfloat16)
        normed_ref[tile * LANES : (tile + 1) * LANES] = normed
        found = lax.dot_general(
            onehot, normed, (((1,), (1,)), ((), ())), preferred_element_type=jnp.float32
        )
        for owner in range(owners):
            picked[owner, tile * slots : (tile + 1) * slots] = found[
                owner * slots : (owner + 1) * slots
            ]

    def second(d, g):
        index = d * n_tm + g
        return pltpu.make_async_remote_copy(
            src_ref=picked.at[partner(d, g)[0]], dst_ref=arrived.at[me],
            send_sem=sems.at[2, index], recv_sem=sems.at[3, index],
            device_id=target(d, g), device_id_type=MESH,
        )

    def second_in(d, g):
        index = d * n_tm + g
        from_chan, from_half = source(d, g)
        return pltpu.make_async_remote_copy(
            src_ref=picked.at[0], dst_ref=arrived.at[from_chan * n_tm + from_half],
            send_sem=sems.at[2, index], recv_sem=sems.at[3, index],
            device_id=target(d, g), device_id_type=MESH,
        )

    for d, g in steps:
        second(d, g).start()
    arrived[me] = picked[chan]
    edge = jnp.zeros((ext_ref.shape[0], LANES), ext_ref.dtype)
    ext_ref[:, :LANES] = edge
    ext_ref[:, LANES + samples :] = edge
    for d, g in steps:
        second_in(d, g).wait_recv()
    for sender in range(n_chan):
        total = arrived[sender * n_tm]
        for other in range(1, n_tm):
            total = total + arrived[sender * n_tm + other]
        for tile in range(samples // LANES):
            wide[
                sender * slots : (sender + 1) * slots, tile * LANES : (tile + 1) * LANES
            ] = total[tile * slots : (tile + 1) * slots]
    ext_ref[:, LANES : LANES + samples] = wide[...].astype(ext_ref.dtype)
    for d, g in steps:
        first(d, g).wait_send()
        second(d, g).wait_send()


def correlate_kernel(scale, ext_ref, normed_ref, out_hbm, out_ref, sems):
    lags, slots, _ = out_ref.shape
    samples = normed_ref.shape[0]
    receivers = normed_ref[...]
    group = max(1, 128 // slots)
    pieces = sems.shape[0]
    piece = group * -(-lags // (group * pieces))
    copies = []
    for start in range(0, lags, group):
        stop = min(start + group, lags)
        windows = []
        for lag in range(start, stop):
            base = LANES + MAXLAG - lag
            windows.append(ext_ref[:, base : base + samples])
        left = jnp.concatenate(windows, axis=0)
        found = jnp.dot(left, receivers, preferred_element_type=jnp.float32) * scale
        out_ref[start:stop] = found.reshape(stop - start, slots, LANES)
        if stop % piece == 0 or stop == lags:
            begin = len(copies) * piece
            copy = pltpu.make_async_copy(
                out_ref.at[begin:stop], out_hbm.at[begin:stop], sems.at[len(copies)]
            )
            copy.start()
            copies.append(copy)
    for copy in copies:
        copy.wait()


def per_device(n_chan, n_tm, raw_strain, fir_taps, source_picks):
    n = n_chan * n_tm
    own = raw_strain.shape[1] // DEC
    rows = own + 8
    samples = own * n
    slots = source_picks.shape[2]
    vmem = pl.BlockSpec(memory_space=pltpu.VMEM)
    anywhere = pl.BlockSpec(memory_space=pl.ANY)
    picks = source_picks.transpose(0, 2, 1)
    traces = n_chan * slots
    normed, ext = pl.pallas_call(
        functools.partial(exchange_kernel, n_chan, n_tm),
        out_shape=(
            jax.ShapeDtypeStruct((samples, LANES), jnp.bfloat16),
            jax.ShapeDtypeStruct((traces, samples + 2 * LANES), jnp.bfloat16),
        ),
        in_specs=[anywhere, anywhere, anywhere],
        out_specs=(vmem, vmem),
        scratch_shapes=[
            pltpu.VMEM((n_chan, raw_strain.shape[1], n_tm * LANES), jnp.bfloat16),
            pltpu.SMEM(fir_taps.shape, jnp.float32),
            pltpu.SMEM(picks.shape, jnp.int32),
            pltpu.VMEM((n, rows, LANES), jnp.float32),
            pltpu.VMEM((n, rows, LANES), jnp.float32),
            pltpu.VMEM((samples + 2 * HALF_WIN, 3 * LANES), jnp.bfloat16),
            pltpu.VMEM((n_chan, slots * samples // LANES, LANES), jnp.float32),
            pltpu.VMEM((n, slots * samples // LANES, LANES), jnp.float32),
            pltpu.VMEM((traces, samples), jnp.float32),
            pltpu.SemaphoreType.DMA((n_chan + 2,)),
            pltpu.SemaphoreType.DMA((4, n)),
        ],
        compiler_params=pltpu.CompilerParams(
            collective_id=0, has_side_effects=True, vmem_limit_bytes=60 * 2**20
        ),
    )(raw_strain, fir_taps, picks)
    out_shape = (2 * MAXLAG + 1, traces, LANES)
    return pl.pallas_call(
        functools.partial(correlate_kernel, 1.0 / math.sqrt(samples)),
        out_shape=jax.ShapeDtypeStruct(out_shape, jnp.float32),
        in_specs=[vmem, vmem],
        out_specs=anywhere,
        scratch_shapes=[
            pltpu.VMEM(out_shape, jnp.float32),
            pltpu.SemaphoreType.DMA((6,)),
        ],
        compiler_params=pltpu.CompilerParams(vmem_limit_bytes=40 * 2**20),
    )(ext, normed)


def solution(mesh):
    placed = (P("tm", "chan", "groups"), P(), P(("groups", "chan"), None, None))
    return jax.shard_map(
        functools.partial(per_device, mesh.shape["chan"], mesh.shape["tm"]),
        mesh=mesh,
        in_specs=placed,
        out_specs=P(None, None, ("groups", "chan", "tm")),
        check_vma=False,
    )
```

time: 28.7 us -> 27.1 us (0.944)
  local copies, waits for them, and re-layouts: 2.72 us -> 1.63 us
  Pallas kernels: 25.8 us -> 25.3 us
    unnamed x5 -> x4, local copies, waits for them, and re-layouts: 2.72 us -> 1.63 us
    pallas_call x1, Pallas kernels: 4.31 us -> 3.92 us  [per_device(): pl.pallas_call(functools.partial(correlate_kernel, 1.0 / math.sqrt(sample...]
where the time goes in v1:
time: 27.1 us; the launch traced here: 26.9 us
  Pallas kernels  25.3 us (93%)
  local copies, waits for them, and re-layouts  1.63 us (6%)
    pallas_call x1, Pallas kernels, per_device(): pl.pallas_call(functools.partial(exchange_kernel, n_chan, n_tm), out_shap...  21.4 us
    pallas_call x1, Pallas kernels, per_device(): pl.pallas_call(functools.partial(correlate_kernel, 1.0 / math.sqrt(sample...  3.92 us
    unnamed x4, local copies, waits for them, and re-layouts  1.63 us

profile of v1, /device:TPU:0, one launch (start us, length us, event | category | flops | bytes accessed | tf_op | source)
XLA Modules:
  0.0 26.9 jit_solution(2343695852679044437)
XLA Ops:
  0.0 21.4 %shard_map.37 = (bf16[512,128]{1,0:T(8,128)(2,1)}, bf16[16,768]{1,0:T(8,128)(2,1)}) custom-call(bf16[1,320,2048]{2,1,0:T(8,128)(2,1)} %raw_hbm.1, f32[64]{0:T(128)} %taps_hbm.1, s32[1,2,8]{2,1,0:T(2,128)} %bitcast.1), custom_call_target="tpu_custom_call" | custom-call | tf_op jit(solution)/shard_map/pallas_call | solution.py:237
  21.4 0.0 copy-start
  21.4 0.9 %copy-done = bf16[512,128]{1,0:T(8,128)(2,1)S(1)} copy-done((bf16[512,128]{1,0:T(8,128)(2,1)S(1)}, bf16[512,128]{1,0:T(8,128)(2,1)}, u32[]{:S(2)}) %copy-start) | copy-done | bytes 131096
  22.3 0.0 copy-start.1
  22.3 0.7 %copy-done.1 = bf16[16,768]{1,0:T(8,128)(2,1)S(1)} copy-done((bf16[16,768]{1,0:T(8,128)(2,1)S(1)}, bf16[16,768]{1,0:T(8,128)(2,1)}, u32[]{:S(2)}) %copy-start.1) | copy-done | bytes 24600
  23.0 3.9 %shard_map.38 = f32[201,16,128]{2,1,0:T(8,128)} custom-call(bf16[16,768]{1,0:T(8,128)(2,1)S(1)} %copy-done.1, bf16[512,128]{1,0:T(8,128)(2,1)S(1)} %copy-done), custom_call_target="tpu_custom_call" | custom-call | tf_op jit(solution)/shard_map/pallas_call | solution.py:263
Async XLA Ops:
  21.4 0.9 %copy-start = (bf16[512,128]{1,0:T(8,128)(2,1)S(1)}, bf16[512,128]{1,0:T(8,128)(2,1)}, u32[]{:S(2)}) copy-start(bf16[512,128]{1,0:T(8,128)(2,1)} %get-tuple-element.8.normed_ref) | copy-start | bytes 393220
  22.3 0.7 %copy-start.1 = (bf16[16,768]{1,0:T(8,128)(2,1)S(1)}, bf16[16,768]{1,0:T(8,128)(2,1)}, u32[]{:S(2)}) copy-start(bf16[16,768]{1,0:T(8,128)(2,1)} %get-tuple-element.7.ext_ref) | copy-start | bytes 73732

commit v2 on v1

--- a/solution.py
+++ b/solution.py
@@ -27,7 +27,8 @@
 
 def exchange_kernel(
     n_chan, n_tm, raw_hbm, taps_hbm, picks_hbm, normed_ref, ext_ref,
-    raw_ref, taps_ref, picks_ref, send, recv, mags, picked, arrived, wide, loads, sems,
+    raw_ref, taps_ref, picks_ref, send, recv, mags, parts, mine, votes,
+    picked, arrived, loads, sems,
 ):
     n = n_chan * n_tm
     chan = lax.axis_index("chan")
@@ -57,9 +58,9 @@
     taps_copy = pltpu.make_async_copy(taps_hbm, taps_ref, loads.at[n_chan])
     picks_copy = pltpu.make_async_copy(picks_hbm, picks_ref, loads.at[n_chan + 1])
     taps_copy.start()
+    picks_copy.start()
     for d in order:
         load(d).start()
-    picks_copy.start()
     barrier = pltpu.get_barrier_semaphore()
     for d, g in steps:
         pl.semaphore_signal(barrier, inc=1, device_id=target(d, g), device_id_type=MESH)
@@ -91,37 +92,97 @@
     for tap in range(TAPS):
         table = jnp.where(tap_index == tap, taps_ref[tap], table)
     weights = jnp.concatenate(split3(table), axis=0)
+    slots, owners = picks_ref.shape[1:]
+    traces = n_chan * slots
+    picks_copy.wait()
+    lane = lax.broadcasted_iota(jnp.int32, mine.shape, 1)
+    vote = jnp.full(mine.shape, -1, jnp.int32)
+    for owner in range(owners):
+        for slot in range(slots):
+            spot = owner * traces + chan * slots + slot
+            vote = jnp.where(lane == spot, picks_ref[0, slot, owner], vote)
+    mine[...] = vote.astype(jnp.float32)
+    votes[0] = mine[...]
+
+    def announce(d):
+        return pltpu.make_async_remote_copy(
+            src_ref=mine, dst_ref=votes.at[d],
+            send_sem=sems.at[4, d], recv_sem=sems.at[5, d],
+            device_id=target(n_chan - d, 0), device_id_type=MESH,
+        )
+
     for place, d in enumerate(order):
         load(d).wait()
         part = jnp.dot(weights, raw_ref[d], preferred_element_type=jnp.float32)
         part = part[:rows] + part[rows : 2 * rows] + part[2 * rows :]
+        parts[d] = jnp.concatenate(split3(part), axis=0)
         for h in range(n_tm):
             send[d * n_tm + h] = part[:, h * LANES : (h + 1) * LANES]
         if place == 0:
             pl.semaphore_wait(barrier, n - 1)
+            for other in range(1, n_chan):
+                announce(other).start()
         for g in range(n_tm):
             if d or g:
                 first(d, g).start()
     recv[my_time] = send[half]
-    picks_copy.wait()
 
     samples = normed_ref.shape[0]
-    mags[:HALF_WIN] = jnp.zeros((HALF_WIN, 3 * LANES), jnp.bfloat16)
-    mags[HALF_WIN + samples :] = jnp.zeros((HALF_WIN, 3 * LANES), jnp.bfloat16)
+    width = mags.shape[1]
+    mags[:HALF_WIN] = jnp.zeros((HALF_WIN, width), jnp.bfloat16)
+    mags[HALF_WIN + samples :] = jnp.zeros((HALF_WIN, width), jnp.bfloat16)
+    mags[HALF_WIN : HALF_WIN + samples, 3 * LANES :] = jnp.zeros(
+        (samples, width - 3 * LANES), jnp.bfloat16
+    )
+    picked[...] = jnp.zeros_like(picked)
+    edge = jnp.zeros((traces, LANES), ext_ref.dtype)
+    ext_ref[:, :LANES] = edge
+    ext_ref[:, LANES + samples :] = edge
+
+    def second(d, g):
+        index = d * n_tm + g
+        return pltpu.make_async_remote_copy(
+            src_ref=picked.at[partner(d, g)[0]], dst_ref=arrived.at[my_time],
+            send_sem=sems.at[2, index], recv_sem=sems.at[3, index],
+            device_id=target(d, g), device_id_type=MESH,
+        )
+
+    def second_in(d, g):
+        index = d * n_tm + g
+        from_chan, from_half = source(d, g)
+        return pltpu.make_async_remote_copy(
+            src_ref=picked.at[0], dst_ref=arrived.at[from_half * n_chan + from_chan],
+            send_sem=sems.at[2, index], recv_sem=sems.at[3, index],
+            device_id=target(d, g), device_id_type=MESH,
+        )
+
+    for d in range(1, n_chan):
+        announce(d).wait_recv()
+    columns = mine.shape[1]
+    position = lax.broadcasted_iota(jnp.int32, (block_width, columns), 0).astype(jnp.float32)
+    found = jnp.zeros((3 * rows, columns), jnp.float32)
+    for d in range(n_chan):
+        onehot = jnp.where(position == votes[d, :1], 1.0, 0.0).astype(jnp.bfloat16)
+        found = found + jnp.dot(parts[d], onehot, preferred_element_type=jnp.float32)
+    found = found[:rows] + found[rows : 2 * rows] + found[2 * rows :]
+    for owner in range(owners):
+        for piece in range(rows // 8):
+            picked[owner, :, piece * traces : (piece + 1) * traces] = found[
+                piece * 8 : (piece + 1) * 8, owner * traces : (owner + 1) * traces
+            ]
+    for d, g in steps:
+        second(d, g).start()
+    arrived[my_time] = picked[chan]
+
     band_shape = (LANES, LANES + 2 * HALF_WIN)
     offset = lax.broadcasted_iota(jnp.int32, band_shape, 1) - lax.broadcasted_iota(
         jnp.int32, band_shape, 0
     )
     band = jnp.where((offset >= 0) & (offset <= 2 * HALF_WIN), 1.0, 0.0).astype(jnp.bfloat16)
-    slots, owners = picks_ref.shape[1:]
-    pick_rows = owners * slots
-    row = lax.broadcasted_iota(jnp.int32, (pick_rows, LANES), 0)
-    lane = lax.broadcasted_iota(jnp.int32, (pick_rows, LANES), 1) + half * LANES
-    chosen = jnp.full((pick_rows, LANES), -1, jnp.int32)
-    for owner in range(owners):
-        for slot in range(slots):
-            chosen = jnp.where(row == owner * slots + slot, picks_ref[0, slot, owner], chosen)
-    onehot = jnp.where(chosen == lane, 1.0, 0.0).astype(jnp.bfloat16)
+    same = lax.broadcasted_iota(jnp.int32, (traces, traces), 0) == lax.broadcasted_iota(
+        jnp.int32, (traces, traces), 1
+    )
+    identity = jnp.where(same, 1.0, 0.0).astype(jnp.bfloat16)
 
     for d, g in steps:
         first_in(d, g).wait_recv()
@@ -133,9 +194,31 @@
         spill = recv[slab - 1, own:]
         return jnp.concatenate([body[: rows - own] + spill, body[rows - own :]], axis=0)
 
+    def source_rows(slab):
+        pieces = [
+            arrived[slab, :, piece * traces : (piece + 1) * traces] for piece in range(own // 8)
+        ]
+        if slab:
+            last = (own // 8) * traces
+            pieces[0] = pieces[0] + arrived[slab - 1, :, last : last + traces]
+        return jnp.concatenate(pieces, axis=0)
+
     for slab in range(n):
         value = jnp.concatenate(split3(jnp.abs(decimated(slab))), axis=1)
-        mags[HALF_WIN + slab * own : HALF_WIN + (slab + 1) * own] = value
+        mags[HALF_WIN + slab * own : HALF_WIN + (slab + 1) * own, : 3 * LANES] = value
+    for d, g in steps:
+        second_in(d, g).wait_recv()
+    for slab in range(n):
+        value = jnp.concatenate(split3(jnp.abs(source_rows(slab))), axis=1)
+        mags[
+            HALF_WIN + slab * own : HALF_WIN + (slab + 1) * own,
+            3 * LANES : 3 * LANES + 3 * traces,
+        ] = value
+
+    def normalized(values, sums):
+        wide = values.shape[1]
+        running = sums[:, :wide] + sums[:, wide : 2 * wide] + sums[:, 2 * wide : 3 * wide]
+        return (values / (running / (2 * HALF_WIN + 1) + epsilon)).astype(jnp.bfloat16)
 
     per_tile = LANES // own
     for tile in range(samples // LANES):
@@ -143,54 +226,19 @@
             band, mags[tile * LANES : tile * LANES + band_shape[1]],
             preferred_element_type=jnp.float32,
         )
-        running = sums[:, :LANES] + sums[:, LANES : 2 * LANES] + sums[:, 2 * LANES :]
-        values = jnp.concatenate(
-            [decimated(tile * per_tile + i) for i in range(per_tile)], axis=0
-        )
-        normed = (values / (running / (2 * HALF_WIN + 1) + epsilon)).astype(jnp.bfloat16)
-        normed_ref[tile * LANES : (tile + 1) * LANES] = normed
-        found = lax.dot_general(
-            onehot, normed, (((1,), (1,)), ((), ())), preferred_element_type=jnp.float32
-        )
-        for owner in range(owners):
-            picked[owner, tile * slots : (tile + 1) * slots] = found[
-                owner * slots : (owner + 1) * slots
-            ]
-
-    def second(d, g):
-        index = d * n_tm + g
-        return pltpu.make_async_remote_copy(
-            src_ref=picked.at[partner(d, g)[0]], dst_ref=arrived.at[me],
-            send_sem=sems.at[2, index], recv_sem=sems.at[3, index],
-            device_id=target(d, g), device_id_type=MESH,
-        )
-
-    def second_in(d, g):
-        index = d * n_tm + g
-        from_chan, from_half = source(d, g)
-        return pltpu.make_async_remote_copy(
-            src_ref=picked.at[0], dst_ref=arrived.at[from_chan * n_tm + from_half],
-            send_sem=sems.at[2, index], recv_sem=sems.at[3, index],
-            device_id=target(d, g), device_id_type=MESH,
-        )
-
-    for d, g in steps:
-        second(d, g).start()
-    arrived[me] = picked[chan]
-    edge = jnp.zeros((ext_ref.shape[0], LANES), ext_ref.dtype)
-    ext_ref[:, :LANES] = edge
-    ext_ref[:, LANES + samples :] = edge
-    for d, g in steps:
-        second_in(d, g).wait_recv()
-    for sender in range(n_chan):
-        total = arrived[sender * n_tm]
-        for other in range(1, n_tm):
-            total = total + arrived[sender * n_tm + other]
-        for tile in range(samples // LANES):
-            wide[
-                sender * slots : (sender + 1) * slots, tile * LANES : (tile + 1) * LANES
-            ] = total[tile * slots : (tile + 1) * slots]
-    ext_ref[:, LANES : LANES + samples] = wide[...].astype(ext_ref.dtype)
+        slabs = range(tile * per_tile, (tile + 1) * per_tile)
+        normed_ref[tile * LANES : (tile + 1) * LANES] = normalized(
+            jnp.concatenate([decimated(slab) for slab in slabs], axis=0), sums[:, : 3 * LANES]
+        )
+        picks = normalized(
+            jnp.concatenate([source_rows(slab) for slab in slabs], axis=0), sums[:, 3 * LANES :]
+        )
+        turned = lax.dot_general(
+            identity, picks, (((1,), (1,)), ((), ())), preferred_element_type=jnp.float32
+        )
+        ext_ref[:, (tile + 1) * LANES : (tile + 2) * LANES] = turned.astype(ext_ref.dtype)
+    for d in range(1, n_chan):
+        announce(d).wait_send()
     for d, g in steps:
         first(d, g).wait_send()
         second(d, g).wait_send()
@@ -234,6 +282,8 @@
     anywhere = pl.BlockSpec(memory_space=pl.ANY)
     picks = source_picks.transpose(0, 2, 1)
     traces = n_chan * slots
+    sum_width = 3 * LANES + pl.cdiv(3 * traces, LANES) * LANES
+    tile_width = pl.cdiv(rows // 8 * traces, LANES) * LANES
     normed, ext = pl.pallas_call(
         functools.partial(exchange_kernel, n_chan, n_tm),
         out_shape=(
@@ -248,12 +298,14 @@
             pltpu.SMEM(picks.shape, jnp.int32),
             pltpu.VMEM((n, rows, LANES), jnp.float32),
             pltpu.VMEM((n, rows, LANES), jnp.float32),
-            pltpu.VMEM((samples + 2 * HALF_WIN, 3 * LANES), jnp.bfloat16),
-            pltpu.VMEM((n_chan, slots * samples // LANES, LANES), jnp.float32),
-            pltpu.VMEM((n, slots * samples // LANES, LANES), jnp.float32),
-            pltpu.VMEM((traces, samples), jnp.float32),
+            pltpu.VMEM((samples + 2 * HALF_WIN, sum_width), jnp.bfloat16),
+            pltpu.VMEM((n_chan, 3 * rows, n_tm * LANES), jnp.bfloat16),
+            pltpu.VMEM((8, n_chan * traces), jnp.float32),
+            pltpu.VMEM((n_chan, 8, n_chan * traces), jnp.float32),
+            pltpu.VMEM((n_chan, 8, tile_width), jnp.float32),
+            pltpu.VMEM((n, 8, tile_width), jnp.float32),
             pltpu.SemaphoreType.DMA((n_chan + 2,)),
-            pltpu.SemaphoreType.DMA((4, n)),
+            pltpu.SemaphoreType.DMA((6, n)),
         ],
         compiler_params=pltpu.CompilerParams(
             collective_id=0, has_side_effects=True, vmem_limit_bytes=60 * 2**20

time: 27.1 us -> 25.3 us (0.934)
  Pallas kernels: 25.3 us -> 23.5 us
    pallas_call x1, Pallas kernels: 21.4 us -> 19.6 us  [per_device(): pl.pallas_call(functools.partial(exchange_kernel, n_chan, n_tm), out_shap...]
where the time goes in v2:
time: 25.3 us; the launch traced here: 25.1 us
  Pallas kernels  23.5 us (93%)
  local copies, waits for them, and re-layouts  1.63 us (6%)
    pallas_call x1, Pallas kernels, per_device(): pl.pallas_call(functools.partial(exchange_kernel, n_chan, n_tm), out_shap...  19.6 us
    pallas_call x1, Pallas kernels, per_device(): pl.pallas_call(functools.partial(correlate_kernel, 1.0 / math.sqrt(sample...  3.92 us
    unnamed x4, local copies, waits for them, and re-layouts  1.63 us

profile of v2, /device:TPU:0, one launch (start us, length us, event | category | flops | bytes accessed | tf_op | source)
XLA Modules:
  0.0 25.1 jit_solution(15232810257317962489)
XLA Ops:
  0.0 19.6 %shard_map.37 = (bf16[512,128]{1,0:T(8,128)(2,1)}, bf16[16,768]{1,0:T(8,128)(2,1)}) custom-call(bf16[1,320,2048]{2,1,0:T(8,128)(2,1)} %raw_hbm.1, f32[64]{0:T(128)} %taps_hbm.1, s32[1,2,8]{2,1,0:T(2,128)} %bitcast.1), custom_call_target="tpu_custom_call" | custom-call | tf_op jit(solution)/shard_map/pallas_call | solution.py:287
  19.6 0.0 copy-start
  19.6 0.9 %copy-done = bf16[512,128]{1,0:T(8,128)(2,1)S(1)} copy-done((bf16[512,128]{1,0:T(8,128)(2,1)S(1)}, bf16[512,128]{1,0:T(8,128)(2,1)}, u32[]{:S(2)}) %copy-start) | copy-done | bytes 131096
  20.5 0.0 copy-start.1
  20.5 0.7 %copy-done.1 = bf16[16,768]{1,0:T(8,128)(2,1)S(1)} copy-done((bf16[16,768]{1,0:T(8,128)(2,1)S(1)}, bf16[16,768]{1,0:T(8,128)(2,1)}, u32[]{:S(2)}) %copy-start.1) | copy-done | bytes 24600
  21.2 3.9 %shard_map.38 = f32[201,16,128]{2,1,0:T(8,128)} custom-call(bf16[16,768]{1,0:T(8,128)(2,1)S(1)} %copy-done.1, bf16[512,128]{1,0:T(8,128)(2,1)S(1)} %copy-done), custom_call_target="tpu_custom_call" | custom-call | tf_op jit(solution)/shard_map/pallas_call | solution.py:315
Async XLA Ops:
  19.6 0.9 %copy-start = (bf16[512,128]{1,0:T(8,128)(2,1)S(1)}, bf16[512,128]{1,0:T(8,128)(2,1)}, u32[]{:S(2)}) copy-start(bf16[512,128]{1,0:T(8,128)(2,1)} %get-tuple-element.8.normed_ref) | copy-start | bytes 393220
  20.5 0.7 %copy-start.1 = (bf16[16,768]{1,0:T(8,128)(2,1)S(1)}, bf16[16,768]{1,0:T(8,128)(2,1)}, u32[]{:S(2)}) copy-start(bf16[16,768]{1,0:T(8,128)(2,1)} %get-tuple-element.7.ext_ref) | copy-start | bytes 73732

commit v3 on v2

--- a/solution.py
+++ b/solution.py
@@ -244,7 +244,13 @@
         second(d, g).wait_send()
 
 
-def correlate_kernel(scale, ext_ref, normed_ref, out_hbm, out_ref, sems):
+def correlate_kernel(scale, ext_hbm, normed_hbm, out_hbm, ext_ref, normed_ref, out_ref, loads, sems):
+    ext_copy = pltpu.make_async_copy(ext_hbm, ext_ref, loads.at[0])
+    normed_copy = pltpu.make_async_copy(normed_hbm, normed_ref, loads.at[1])
+    ext_copy.start()
+    normed_copy.start()
+    ext_copy.wait()
+    normed_copy.wait()
     lags, slots, _ = out_ref.shape
     samples = normed_ref.shape[0]
     receivers = normed_ref[...]
@@ -315,13 +321,16 @@
     return pl.pallas_call(
         functools.partial(correlate_kernel, 1.0 / math.sqrt(samples)),
         out_shape=jax.ShapeDtypeStruct(out_shape, jnp.float32),
-        in_specs=[vmem, vmem],
+        in_specs=[anywhere, anywhere],
         out_specs=anywhere,
         scratch_shapes=[
+            pltpu.VMEM(ext.shape, ext.dtype),
+            pltpu.VMEM(normed.shape, normed.dtype),
             pltpu.VMEM(out_shape, jnp.float32),
+            pltpu.SemaphoreType.DMA((2,)),
             pltpu.SemaphoreType.DMA((6,)),
         ],
-        compiler_params=pltpu.CompilerParams(vmem_limit_bytes=40 * 2**20),
+        compiler_params=pltpu.CompilerParams(vmem_limit_bytes=60 * 2**20),
     )(ext, normed)
 
 

time: 25.3 us -> 24.6 us (0.972)
  local copies, waits for them, and re-layouts: 1.63 us -> 0 us
  Pallas kernels: 23.5 us -> 24.4 us
    unnamed x4 -> x0, local copies, waits for them, and re-layouts: 1.63 us -> none
    pallas_call x1, Pallas kernels: 3.92 us -> 4.85 us  [per_device(): pl.pallas_call(functools.partial(correlate_kernel, 1.0 / math.sqrt(sample...]
where the time goes in v3:
time: 24.6 us; the launch traced here: 24.4 us
  Pallas kernels  24.4 us (99%)
    pallas_call x1, Pallas kernels, per_device(): pl.pallas_call(functools.partial(exchange_kernel, n_chan, n_tm), out_shap...  19.6 us
    pallas_call x1, Pallas kernels, per_device(): pl.pallas_call(functools.partial(correlate_kernel, 1.0 / math.sqrt(sample...  4.85 us

profile of v3, /device:TPU:0, one launch (start us, length us, event | category | flops | bytes accessed | tf_op | source)
XLA Modules:
  0.0 24.4 jit_solution(3770897875671961775)
XLA Ops:
  0.0 19.6 %shard_map.37 = (bf16[512,128]{1,0:T(8,128)(2,1)}, bf16[16,768]{1,0:T(8,128)(2,1)}) custom-call(bf16[1,320,2048]{2,1,0:T(8,128)(2,1)} %raw_hbm.1, f32[64]{0:T(128)} %taps_hbm.1, s32[1,2,8]{2,1,0:T(2,128)} %bitcast.1), custom_call_target="tpu_custom_call" | custom-call | tf_op jit(solution)/shard_map/pallas_call | solution.py:293
  19.6 4.9 %shard_map.38 = f32[201,16,128]{2,1,0:T(8,128)} custom-call(bf16[16,768]{1,0:T(8,128)(2,1)} %get-tuple-element.7.ext_hbm, bf16[512,128]{1,0:T(8,128)(2,1)} %get-tuple-element.8.normed_hbm), custom_call_target="tpu_custom_call" | custom-call | tf_op jit(solution)/shard_map/pallas_call | solution.py:321
